TPU v7x, 128 devices: a whole 4x4x4 slice. The times are simulated.
128 devices in a mesh: tm: 8 (over x, z_hi), clip: 16 (over z_lo, y, core).
Axes of the slice: x: 4, y: 4, z: 4 (z_hi: 2, z_lo: 2; z = z_hi * 2 + z_lo), core: 2. Of those that a mesh axis runs over, the one named last changes fastest.
Arguments:
- frame_tokens: bfloat16 [64, 8, 256, 512], P('clip', 'tm'), may hold values from -6 to 6
- actions: int32 [64, 8], P('clip', 'tm'), may hold values from 0 to 7
- frame_counts: int32 [64], P('clip'), may hold values from 2 to 8, as said below
- action_table: bfloat16 [8, 512], replicated, may hold values from -6 to 6
- ln_gain: float32 [3, 512], replicated, may hold values from 0.5 to 1.5
- ln_bias: float32 [3, 512], replicated, may hold values from -1.2 to 1.2
- w_sqkv: bfloat16 [512, 1536], replicated, may hold values from -0.25 to 0.25
- w_so: bfloat16 [512, 512], replicated, may hold values from -2 to 2
- w_tqkv: bfloat16 [512, 1536], replicated, may hold values from -0.25 to 0.25
- w_to: bfloat16 [512, 512], replicated, may hold values from -0.375 to 0.375
- w_up: bfloat16 [512, 2048], replicated, may hold values from -0.25 to 0.25
- b_up: float32 [2048], replicated, may hold values from -3 to 3
- w_down: bfloat16 [2048, 512], replicated, may hold values from -0.125 to 0.125
- cotangent: bfloat16 [64, 8, 256, 512], P('clip', 'tm'), may hold values from -6 to 6
Outputs:
- block_out: bfloat16 [64, 8, 256, 512], P('clip', 'tm')
- grad_input: float32 [64, 8, 256, 512], P('clip', 'tm')
- grad_table: float32 [8, 512], replicated
- grad_gain: float32 [3, 512], replicated
- grad_bias: float32 [3, 512], replicated
- grad_sqkv: float32 [512, 1536], replicated
- grad_so: float32 [512, 512], replicated
- grad_tqkv: float32 [512, 1536], replicated
- grad_to: float32 [512, 512], replicated
- grad_up: float32 [512, 2048], replicated
- up_bias_gradient: float32 [2048], replicated
- grad_down: float32 [2048, 512], replicated
Inputs may be any that keep to these rules, and one draw needn't show every extreme that they name: `frame_counts`: frames present in a clip come first in it; in each aligned block of 4 clips one clip holds all 8 frames.
All inputs are finite; a program needn't handle non-finite values.
Results may differ from a plain program's by a relative error of at most 0.014.
Values may be sent and summed in bfloat16 or wider, within the bound.
No kernel may reach another device: no remote copies, remote signals or barrier semaphores. Data moves between devices by JAX's collectives and lax.ppermute only.
A program may use at most 256 MiB of HBM per device.

v0:
```python
import math
import jax
import jax.numpy as jnp
from jax import lax
from jax.sharding import PartitionSpec as P

HEADS = 8
eps_norm = 1e-05
big_negative = -1e30


def layer_norm(values, gain_row, shift_row):
    center = values - jnp.mean(values, axis=-1, keepdims=True)
    spread = jnp.mean(center * center, axis=-1, keepdims=True)
    return center * lax.rsqrt(spread + eps_norm) * gain_row + shift_row


def norm_back(values, gain_row, shift_row, upstream):
    _, pull = jax.vjp(layer_norm, values, gain_row, shift_row)
    return pull(upstream)


def right_mul(values, weight):
    return jnp.dot(values, weight, preferred_element_type=jnp.float32)


def backward_multiply(values, weight):
    return lax.dot_general(
        values, weight, (((values.ndim - 1,), (1,)), ((), ())), preferred_element_type=jnp.float32
    )


def weight_gradient(left_side, right_side):
    left_flat = left_side.reshape(-1, left_side.shape[-1])
    right_flat = right_side.reshape(-1, right_side.shape[-1])
    return lax.dot_general(
        left_flat, right_flat, (((0,), (0,)), ((), ())), preferred_element_type=jnp.float32
    )


def shards(
    frame_tokens,
    actions,
    frame_counts,
    action_table,
    ln_gain,
    ln_bias,
    w_sqkv,
    w_so,
    w_tqkv,
    w_to,
    w_up,
    b_up,
    w_down,
    cotangent,
):
    clip_count, frames_here, patch_len, model_width = frame_tokens.shape
    head_count = HEADS
    head_dim = model_width // head_count
    score_scale = 1.0 / math.sqrt(head_dim)
    frame_rows = clip_count * frames_here
    frames_all = frames_here * lax.axis_size("tm")
    frame_ids = lax.axis_index("tm") * frames_here + jnp.arange(frames_here, dtype=jnp.int32)
    key_ids = jnp.arange(frames_all, dtype=jnp.int32)
    frame_mask = (frame_ids[None, :] < frame_counts[:, None]).astype(jnp.float32)
    allowed = (key_ids[None, None, :] < frame_counts[:, None, None]) & (
        key_ids[None, None, :] <= frame_ids[None, :, None]
    )
    allowed = allowed[:, None, None, :, :]
    onehot = (actions[..., None] == jnp.arange(action_table.shape[0], dtype=jnp.int32)).astype(
        jnp.float32
    )
    embedded = jnp.einsum(
        "cfa,ad->cfd", onehot, action_table.astype(jnp.float32), precision=lax.Precision.HIGHEST
    )
    first_state = frame_tokens.astype(jnp.float32) + embedded[:, :, None, :]
    act_one = layer_norm(first_state, ln_gain[0], ln_bias[0]).astype(jnp.bfloat16)
    s_qkv = (
        right_mul(act_one, w_sqkv)
        .astype(jnp.bfloat16)
        .reshape(frame_rows, patch_len, 3, head_count, head_dim)
    )
    s_query, s_key, s_value = (s_qkv[:, :, 0], s_qkv[:, :, 1], s_qkv[:, :, 2])
    s_scores = (
        jnp.einsum("nphd,nqhd->nhpq", s_query, s_key, preferred_element_type=jnp.float32)
        * score_scale
    )
    s_probs = jax.nn.softmax(s_scores, axis=-1)
    s_low = s_probs.astype(jnp.bfloat16)
    s_out = jnp.einsum(
        "nhpq,nqhd->nphd", s_low, s_value, preferred_element_type=jnp.float32
    ).astype(jnp.bfloat16)
    s_out = s_out.reshape(clip_count, frames_here, patch_len, model_width)
    mid_state = first_state + right_mul(s_out, w_so)
    act_two = layer_norm(mid_state, ln_gain[1], ln_bias[1]).astype(jnp.bfloat16)
    t_qkv = right_mul(act_two, w_tqkv).astype(jnp.bfloat16)
    t_query = t_qkv[..., :model_width].reshape(
        clip_count, frames_here, patch_len, head_count, head_dim
    )
    kv_local = t_qkv[..., model_width:]
    whole = lax.all_gather(kv_local, "tm", axis=1, tiled=True)
    frame_total = whole.shape[1]
    key_part = whole[..., :model_width].reshape(
        clip_count, frame_total, patch_len, head_count, head_dim
    )
    value_part = whole[..., model_width:].reshape(
        clip_count, frame_total, patch_len, head_count, head_dim
    )
    t_scores = (
        jnp.einsum("cfphd,cephd->cphfe", t_query, key_part, preferred_element_type=jnp.float32)
        * score_scale
    )
    t_scores = jnp.where(allowed, t_scores, big_negative)
    t_probs = jax.nn.softmax(t_scores, axis=-1)
    t_low = t_probs.astype(jnp.bfloat16)
    t_out = jnp.einsum(
        "cphfe,cephd->cfphd", t_low, value_part, preferred_element_type=jnp.float32
    ).astype(jnp.bfloat16)
    t_out = t_out.reshape(clip_count, frames_here, patch_len, model_width)
    late_state = mid_state + right_mul(t_out, w_to)
    act_three = layer_norm(late_state, ln_gain[2], ln_bias[2]).astype(jnp.bfloat16)
    pre_act = right_mul(act_three, w_up) + b_up
    hidden = jax.nn.gelu(pre_act).astype(jnp.bfloat16)
    block_out = (late_state + right_mul(hidden, w_down)).astype(jnp.bfloat16)
    d_out = cotangent.astype(jnp.float32) * frame_mask[:, :, None, None]
    d_down = d_out.astype(jnp.bfloat16)
    grad_down = weight_gradient(hidden, d_down)
    d_hidden = backward_multiply(d_down, w_down)
    _, gelu_pull = jax.vjp(jax.nn.gelu, pre_act)
    d_pre = gelu_pull(d_hidden)[0].astype(jnp.bfloat16)
    grad_up = weight_gradient(act_three, d_pre)
    up_bias_gradient = jnp.sum(d_pre.astype(jnp.float32), axis=(0, 1, 2))
    d_norm3, gain_three, bias_three = norm_back(
        late_state, ln_gain[2], ln_bias[2], backward_multiply(d_pre, w_up)
    )
    d_late = d_out + d_norm3
    ffn_part = (grad_up, up_bias_gradient, grad_down, gain_three, bias_three)
    d_tproj = d_late.astype(jnp.bfloat16)
    grad_to = weight_gradient(t_out, d_tproj)
    d_tout = (
        backward_multiply(d_tproj, w_to)
        .astype(jnp.bfloat16)
        .reshape(clip_count, frames_here, patch_len, head_count, head_dim)
    )
    d_tprob = jnp.einsum(
        "cfphd,cephd->cphfe", d_tout, value_part, preferred_element_type=jnp.float32
    )
    t_delta = jnp.sum(t_probs * d_tprob, axis=-1, keepdims=True)
    d_tscore = (t_probs * (d_tprob - t_delta)).astype(jnp.bfloat16)
    d_tquery = (
        jnp.einsum("cphfe,cephd->cfphd", d_tscore, key_part, preferred_element_type=jnp.float32)
        * score_scale
    )
    row_count = frames_here * lax.axis_size("tm")
    d_key = (
        jnp.einsum("cphfe,cfphd->ecphd", d_tscore, t_query, preferred_element_type=jnp.float32)
        * score_scale
    )
    d_value = jnp.einsum("cphfe,cfphd->ecphd", t_low, d_tout, preferred_element_type=jnp.float32)
    d_kv = lax.psum_scatter(
        jnp.concatenate(
            [
                d_key.reshape(row_count, clip_count, patch_len, model_width),
                d_value.reshape(row_count, clip_count, patch_len, model_width),
            ],
            axis=-1,
        ).astype(jnp.bfloat16),
        "tm",
        scatter_dimension=0,
        tiled=True,
    ).astype(jnp.float32)
    d_kv = jnp.transpose(d_kv, (1, 0, 2, 3))
    d_tqkv = jnp.concatenate(
        [d_tquery.reshape(clip_count, frames_here, patch_len, model_width), d_kv], axis=-1
    ).astype(jnp.bfloat16)
    grad_tqkv = weight_gradient(act_two, d_tqkv)
    d_norm2, gain_two, bias_two = norm_back(
        mid_state, ln_gain[1], ln_bias[1], backward_multiply(d_tqkv, w_tqkv)
    )
    d_mid = d_late + d_norm2
    temporal_part = (grad_tqkv, grad_to, gain_two, bias_two)
    d_sproj = d_mid.astype(jnp.bfloat16)
    grad_so = weight_gradient(s_out, d_sproj)
    d_sout = (
        backward_multiply(d_sproj, w_so)
        .astype(jnp.bfloat16)
        .reshape(frame_rows, patch_len, head_count, head_dim)
    )
    d_sprob = jnp.einsum("nphd,nqhd->nhpq", d_sout, s_value, preferred_element_type=jnp.float32)
    s_delta = jnp.sum(s_probs * d_sprob, axis=-1, keepdims=True)
    d_sscore = (s_probs * (d_sprob - s_delta)).astype(jnp.bfloat16)
    spatial_query_gradient = (
        jnp.einsum("nhpq,nqhd->nphd", d_sscore, s_key, preferred_element_type=jnp.float32)
        * score_scale
    )
    spatial_key_gradient = (
        jnp.einsum("nhpq,nphd->nqhd", d_sscore, s_query, preferred_element_type=jnp.float32)
        * score_scale
    )
    spatial_value_gradient = jnp.einsum(
        "nhpq,nphd->nqhd", s_low, d_sout, preferred_element_type=jnp.float32
    )
    spatial_projection_gradient = jnp.stack(
        [spatial_query_gradient, spatial_key_gradient, spatial_value_gradient], axis=2
    ).reshape(clip_count, frames_here, patch_len, 3 * model_width)
    spatial_projection_gradient = spatial_projection_gradient.astype(jnp.bfloat16)
    grad_sqkv = weight_gradient(act_one, spatial_projection_gradient)
    d_norm1, gain_one, bias_one = norm_back(
        first_state, ln_gain[0], ln_bias[0], backward_multiply(spatial_projection_gradient, w_sqkv)
    )
    grad_input = d_mid + d_norm1
    frame_sums = jnp.sum(grad_input, axis=2)
    grad_table = jnp.einsum("cfa,cfd->ad", onehot, frame_sums, precision=lax.Precision.HIGHEST)
    spatial_part = (grad_sqkv, grad_so, gain_one, bias_one, grad_table)
    summed = ffn_part + temporal_part + spatial_part
    summed = lax.psum(summed, ("tm", "clip"))
    (
        grad_up,
        up_bias_gradient,
        grad_down,
        gain_three,
        bias_three,
        grad_tqkv,
        grad_to,
        gain_two,
        bias_two,
        grad_sqkv,
        grad_so,
        gain_one,
        bias_one,
        grad_table,
    ) = summed
    grad_gain = jnp.stack([gain_one, gain_two, gain_three], axis=0)
    grad_bias = jnp.stack([bias_one, bias_two, bias_three], axis=0)
    return (
        block_out,
        grad_input,
        grad_table,
        grad_gain,
        grad_bias,
        grad_sqkv,
        grad_so,
        grad_tqkv,
        grad_to,
        grad_up,
        up_bias_gradient,
        grad_down,
    )


def solution(mesh):
    in_specs = (
        P("clip", "tm", None, None),
        P("clip", "tm"),
        P("clip"),
        P(),
        P(),
        P(),
        P(),
        P(),
        P(),
        P(),
        P(),
        P(),
        P(),
        P("clip", "tm", None, None),
    )
    out_specs = (
        P("clip", "tm", None, None),
        P("clip", "tm", None, None),
        P(),
        P(),
        P(),
        P(),
        P(),
        P(),
        P(),
        P(),
        P(),
        P(),
    )
    return jax.shard_map(shards, mesh=mesh, in_specs=in_specs, out_specs=out_specs, check_vma=False)
```

profile of v0, /device:TPU:1, one launch (start us, length us, event | category | flops | bytes accessed | tf_op | source)
XLA Modules:
  0.0 842.0 jit_solution(15253249235514504297)
XLA Ops:
  14.3 5.0 convolution_convert_fusion.1
  26.8 6.3 fusion.101
  51.0 182.7 %all-gather.2.cloned.1.call-done = bf16[4,8,256,1024]{3,2,0,1:T(8,128)(2,1)} async-done(((bf16[4,1,256,1024]{3,2,0,1:T(8,128)(2,1)}), bf16[4,8,256,1024]{3,2,0,1:T(8,128)(2,1)}) %all-gather.2.cloned.1.call-update) | async-done | bytes 16777232 | tf_op jit(solution)/shard_map/all_gather | solution.py:101
  233.7 11.5 %fusion.98 = (bf16[4,8,256,512]{3,2,0,1:T(8,128)(2,1)}, bf16[4,8,256,512]{3,2,0,1:T(8,128)(2,1)}) fusion(bf16[4,8,256,1024]{3,2,0,1:T(8,128)(2,1)} %all-gather.2.cloned.1.call-done), kind=kLoop, calls=%fused_computation.157 | loop fusion | bytes 33554432 | tf_op jit(solution)/shard_map/slice | solution.py:103
  245.2 11.4 %copy.148 = bf16[4,8,256,512]{2,3,1,0:T(8,128)(2,1)} copy(bf16[4,8,256,512]{3,2,0,1:T(8,128)(2,1)} %get-tuple-element.72) | data formatting | bytes 16777216
  256.6 7.4 multiply_reduce_fusion.3
  265.1 11.4 %copy.147 = bf16[4,8,256,512]{2,3,1,0:T(8,128)(2,1)} copy(bf16[4,8,256,512]{3,2,0,1:T(8,128)(2,1)} %get-tuple-element.73) | data formatting | bytes 16777216
  276.4 6.0 multiply_reduce_fusion.2
  288.2 8.0 convert_reduce_fusion
  309.0 7.6 multiply_reduce_fusion.1
  316.9 5.6 multiply_convert_fusion.1
  322.6 12.2 %copy.88 = bf16[8,4,256,512]{3,2,1,0:T(8,128)(2,1)} copy(bf16[8,4,256,512]{2,3,1,0:T(8,128)(2,1)} %bitcast.271) | data formatting | bytes 16777216 | tf_op jit(solution)/shard_map/reshape | solution.py:163
  334.8 8.7 %multiply_convert_fusion = bf16[4,256,8,64,8]{1,3,2,0,4:T(8,128)(2,1)} fusion(f32[4,256,8,8]{1,2,0,3:T(8,128)S(1)} %copy-done.35, f32[4,256,8,64]{1,3,2,0:T(8,128)} %copy-done.13), kind=kLoop, calls=%fused_computation.6 | loop fusion | flops 8388608 | bytes 10747904 | tf_op jit(solution)/shard_map/convert.11
  343.4 12.1 %copy.89 = bf16[8,4,256,512]{3,2,1,0:T(8,128)(2,1)} copy(bf16[8,4,256,512]{2,3,1,0:T(8,128)(2,1)} %bitcast.270) | data formatting | bytes 16777216 | tf_op jit(solution)/shard_map/reshape | solution.py:164
  355.6 14.0 %pad_maximum_fusion = bf16[8,4,256,1024]{3,2,1,0:T(8,128)(2,1)} fusion(bf16[8,4,256,512]{3,2,1,0:T(8,128)(2,1)} %copy.89, bf16[8,4,256,512]{3,2,1,0:T(8,128)(2,1)} %copy.88), kind=kLoop, calls=%fused_computation.1 | loop fusion | flops 33554432 | bytes 33554432 | tf_op jit(solution)/shard_map/concatenate | solution.py:161
  375.0 6.8 multiply_reduce_fusion
  386.8 6.9 convolution_bitcast_fusion.3
  393.8 9.9 %convolution_bitcast_fusion.2 = f32[2048,512]{1,0:T(8,128)} fusion(bf16[4,1,256,512]{3,2,1,0:T(8,128)(2,1)S(1)} %copy-done.21, f32[4]{0:T(128)S(1)} %copy-done.48, f32[4,256,2048]{2,1,0:T(8,128)} %copy-done.63, f32[2048]{0:T(1024)S(1)} %copy-done.61), kind=kOutput, calls=%fused_computation.32 | convolution fusion | flops 2170028032 | bytes 13639696 | tf_op jit(solution)/shard_map/dot_general | solution.py:36
  403.6 154.7 %reduce-scatter.2.cloned.1.call-done = bf16[1,4,256,1024]{3,2,1,0:T(8,128)(2,1)} async-done(((bf16[8,4,256,1024]{3,2,1,0:T(8,128)(2,1)}), bf16[1,4,256,1024]{3,2,1,0:T(8,128)(2,1)}) %reduce-scatter.2.cloned.1.call-update) | async-done | bytes 2097168 | tf_op jit(solution)/shard_map/reduce_scatter | solution.py:160
  558.3 5.1 fusion.17
  597.9 8.1 fusion.52
  608.4 5.8 fusion.16
  622.9 68.0 %all-reduce = (f32[8,512]{1,0:T(8,128)}, f32[1,512]{1,0:T(1,128)S(1)}, f32[1,512]{1,0:T(1,128)S(1)}, f32[1,512]{1,0:T(1,128)S(1)}, f32[1,512]{1,0:T(1,128)S(1)},...) all-reduce(f32[8,512]{1,0:T(8,128)S(1)} %fusion.88, ...), channel_id=1, replica_groups=mesh['tm'=8,'clip'=16] {'tm','clip'}, use_global_device_ids=true, to_apply=%region_20.21 | all-reduce | flops 9216 | bytes 73728 | tf_op jit(solution)/shard_map/psum | solution.py:216
  691.5 128.9 %all-reduce.4.cloned.1.call-done = (f32[512,1536]{1,0:T(8,128)}, f32[512,512]{1,0:T(8,128)}, f32[512,1536]{1,0:T(8,128)}, f32[512,512]{1,0:T(8,128)}, f32[512,2048]{1,0:T(8,128)}, /*index=5*/f32[2048,512]{1,0:T(8,128)}) async-done(((f32[512,1536]{1,0:T(8,128)}, f32[512,512]{1,0:T(8,128)}, f32[512,1536]{1,0:T(8,128)}, f32[512,512]{1,0:T(8,128)}, f32[512,2048]{1,0:T(8,128)}, ...) | async-done | bytes 16777232 | tf_op jit(solution)/shard_map/psum | solution.py:216
  (217 shorter events, 123.0 us)
Async XLA Ops:
  7.2 280.9 %copy-start = (bf16[2048,512]{1,0:T(8,128)(2,1)S(1)}, bf16[2048,512]{1,0:T(8,128)(2,1)}, u32[]{:S(2)}) copy-start(bf16[2048,512]{1,0:T(8,128)(2,1)} %param.26) | copy-start | bytes 6291460
  7.2 7.2 copy-start.14
  7.2 226.5 %all-gather.2.cloned.1.call-start = ((), (), s32[]{:S(2)}) async-start(), calls=%async_computation.1 | async-start | bytes 18874368 | tf_op jit(solution)/shard_map/all_gather | solution.py:101
  8.2 11.2 %copy-start.45 = (f32[1,512]{1,0:T(1,128)}, f32[1,512]{1,0:T(1,128)S(1)}, u32[]{:S(2)}) copy-start(f32[1,512]{1,0:T(1,128)S(1)} %get-tuple-element.76) | copy-start | bytes 6148
  9.0 10.4 %copy-start.50 = (f32[1,512]{1,0:T(1,128)}, f32[1,512]{1,0:T(1,128)S(1)}, u32[]{:S(2)}) copy-start(f32[1,512]{1,0:T(1,128)S(1)} %get-tuple-element.79) | copy-start | bytes 6148
  9.0 28.9 %copy-start.52 = (f32[1,512]{1,0:T(1,128)}, f32[1,512]{1,0:T(1,128)S(1)}, u32[]{:S(2)}) copy-start(f32[1,512]{1,0:T(1,128)S(1)} %get-tuple-element.80) | copy-start | bytes 6148
  9.9 26.6 %copy-start.37 = (f32[4,512]{1,0:T(4,128)}, f32[4,512]{1,0:T(4,128)S(1)}, u32[]{:S(2)}) copy-start(f32[4,512]{1,0:T(4,128)S(1)} %fusion.89) | copy-start | bytes 24580
  44.8 513.5 %reduce-scatter.2.cloned.1.call-start = ((), (), s32[]{:S(2)}) async-start(), calls=%async_computation.2 | async-start | bytes 18874368 | tf_op jit(solution)/shard_map/reduce_scatter | solution.py:160
  276.4 6.0 copy-start.3
  276.4 6.0 copy-start.36
  283.3 16.2 %copy-start.5 = (f32[4,1,256,512]{3,2,0,1:T(8,128)}, f32[4,1,256,512]{3,2,0,1:T(8,128)S(1)}, u32[]{:S(2)}) copy-start(f32[4,1,256,512]{3,2,0,1:T(8,128)S(1)} %get-tuple-element.86) | copy-start | bytes 6291460
  288.1 8.0 copy-start.63
  309.0 7.6 copy-start.13
  309.0 7.9 copy-start.12
  316.9 5.7 copy-start.25
  322.6 12.2 %copy-start.35 = (f32[4,256,8,8]{1,2,0,3:T(8,128)S(1)}, f32[4,256,8,8]{1,2,0,3:T(8,128)}, u32[]{:S(2)}) copy-start(f32[4,256,8,8]{1,2,0,3:T(8,128)} %convert_convert_fusion) | copy-start | bytes 786436
  369.6 450.8 %all-reduce.4.cloned.1.call-start = ((), (), s32[]{:S(2)}) async-start(), calls=%async_computation.3 | async-start | bytes 33554432 | tf_op jit(solution)/shard_map/psum | solution.py:216
  386.8 6.9 copy-start.21
  386.8 6.9 copy-start.48
  386.8 6.9 copy-start.61
  558.3 5.1 copy-start.32
  558.3 5.1 copy-start.53
  558.3 5.1 copy-start.56
  575.2 9.4 %slice-start = ((s8[8388608]{0:T(1024)(128)(4,1)}), s8[4194304]{0:T(1024)(128)(4,1)S(1)}, s32[]{:S(2)}) async-start(s8[8388608]{0:T(1024)(128)(4,1)} %bitcast.268), calls=%async_computation.4 | async-start | bytes 8388608
  (45 other events, 118.6 us)
Sparse Core Ops, SparseCore 0:
  44.9 188.7 all-gather.1
  369.7 188.5 reduce-scatter.1
  596.3 224.0 all-reduce.3
where the time goes:
time: 850 us; the launch traced here: 842 us
  waiting for transfers between devices  466 us (55%)
  local copies, waits for them, and re-layouts  108 us (13%)
  matrix products  92.8 us (11%)
  other arithmetic  91.3 us (11%)
  blocking collectives  68 us (8%)
  between operations  14.9 us (2%)
    all_gather x1, waiting for transfers between devices, shards(): whole = lax.all_gather(kv_local, 'tm', axis=1, tiled=True)  183 us
    reduce_scatter x1, waiting for transfers between devices, shards(): lax.psum_scatter(jnp.concatenate([d_key.reshape(row_count, clip_count, pa...  155 us
    psum x1, waiting for transfers between devices, shards(): summed = lax.psum(summed, ('tm', 'clip'))  129 us
    psum x1, blocking collectives, shards(): summed = lax.psum(summed, ('tm', 'clip'))  68 us
    unnamed x142, local copies, waits for them, and re-layouts  51.7 us
    dot_general x6, matrix products, weight_gradient(): lax.dot_general(left_flat, right_flat, (((0,), (0,)), ((), ())), preferre...  29.4 us
    dot_general x6, matrix products, backward_multiply(): lax.dot_general(values, weight, (((values.ndim - 1,), (1,)), ((), ())), p...  25.7 us
    dot_general x6, matrix products, right_mul(): return jnp.dot(values, weight, preferred_element_type=jnp.float32)  19.1 us
  transfers between devices with their start and end apart: 3, of which 3 were waited for; matrix products, arithmetic and copies ran while one was open for 8% of the time, Pallas kernels for 0%

commit v1 on v0

--- a/solution.py
+++ b/solution.py
@@ -98,7 +98,9 @@
         clip_count, frames_here, patch_len, head_count, head_dim
     )
     kv_local = t_qkv[..., model_width:]
-    whole = lax.all_gather(kv_local, "tm", axis=1, tiled=True)
+    whole = jnp.concatenate(
+        lax.all_to_all(jnp.stack([kv_local] * lax.axis_size("tm")), "tm", 0, 0), axis=1
+    )
     frame_total = whole.shape[1]
     key_part = whole[..., :model_width].reshape(
         clip_count, frame_total, patch_len, head_count, head_dim

time: 850 us -> 900 us (1.059)
  waiting for transfers between devices: 466 us -> 509 us
    all_to_all x0 -> x1, waiting for transfers between devices: none -> 221 us  [shards(): lax.all_to_all(jnp.stack([kv_local] * lax.axis_size('tm')), 'tm', 0, 0)]
    all_gather x1 -> x0, waiting for transfers between devices: 183 us -> none  [shards(): whole = lax.all_gather(kv_local, 'tm', axis=1, tiled=True)]
    unnamed x142 -> x132, local copies, waits for them, and re-layouts: 51.7 us -> 29 us
    all_to_all x0 -> x1, local copies, waits for them, and re-layouts: none -> 13.8 us  [shards(): lax.all_to_all(jnp.stack([kv_local] * lax.axis_size('tm')), 'tm', 0, 0)]
  transfers between devices with their start and end apart: 3 -> 3, of which waited for: 3 -> 3; matrix products, arithmetic and copies ran while one was open for 8% -> 7% of each run, Pallas kernels for 0% -> 0%
where the time goes in v1:
time: 900 us; the launch traced here: 892 us
  waiting for transfers between devices  509 us (57%)
  local copies, waits for them, and re-layouts  105 us (12%)
  other arithmetic  94.2 us (10%)
  matrix products  92 us (10%)
  blocking collectives  67.9 us (8%)
  between operations  15 us (2%)
  starting transfers between devices  9.16 us (1%)
    all_to_all x1, waiting for transfers between devices, shards(): lax.all_to_all(jnp.stack([kv_local] * lax.axis_size('tm')), 'tm', 0, 0)  221 us
    reduce_scatter x1, waiting for transfers between devices, shards(): lax.psum_scatter(jnp.concatenate([d_key.reshape(row_count, clip_count, pa...  159 us
    psum x1, waiting for transfers between devices, shards(): summed = lax.psum(summed, ('tm', 'clip'))  129 us
    psum x1, blocking collectives, shards(): summed = lax.psum(summed, ('tm', 'clip'))  67.9 us
    dot_general x6, matrix products, weight_gradient(): lax.dot_general(left_flat, right_flat, (((0,), (0,)), ((), ())), preferre...  29.3 us
    unnamed x132, local copies, waits for them, and re-layouts  29 us
    dot_general x6, matrix products, backward_multiply(): lax.dot_general(values, weight, (((values.ndim - 1,), (1,)), ((), ())), p...  25.1 us
    unnamed x7, other arithmetic  23 us
  transfers between devices with their start and end apart: 3, of which 3 were waited for; matrix products, arithmetic and copies ran while one was open for 7% of the time, Pallas kernels for 0%

profile of v1, /device:TPU:1, one launch (start us, length us, event | category | flops | bytes accessed | tf_op | source)
XLA Modules:
  0.0 892.1 jit_solution(6932033348919513040)
XLA Ops:
  26.7 6.3 fusion.100
  48.6 6.8 stack.47
  55.4 8.2 all-to-all-start
  69.6 221.5 %all-to-all-done = bf16[8,4,1,256,1024]{3,4,1,2,0:T(8,128)(2,1)} async-done(((bf16[8,4,1,256,1024]{3,4,1,2,0:T(8,128)(2,1)}), bf16[8,4,1,256,1024]{3,4,1,2,0:T(8,128)(2,1)}, u32[]{:S(2)}, u32[]{:S(2)}) %all-to-all-start) | async-done | bytes 16777248 | tf_op jit(solution)/shard_map/all_to_all | solution.py:102
  291.0 13.8 %copy.180 = bf16[8,4,1,256,1024]{3,4,0,1,2:T(8,128)(2,1)} copy(bf16[8,4,1,256,1024]{3,4,1,2,0:T(8,128)(2,1)} %all-to-all-done) | data formatting | bytes 33554432 | tf_op jit(solution)/shard_map/all_to_all | solution.py:102
  304.8 7.5 slice.62
  312.3 11.5 %multiply_reduce_fusion.3 = (f32[4,256,8,8]{1,2,3,0:T(8,128)S(1)}, bf16[4,8,256,512]{2,3,1,0:T(8,128)(2,1)}) fusion(f32[4,256,8,64]{1,3,2,0:T(8,128)} %convert.35, bf16[4,8,256,1024]{2,3,1,0:T(8,128)(2,1)} %bitcast.274), kind=kLoop, calls=%fused_computation.5 | loop fusion | flops 12517376 | bytes 19136512
  324.8 6.0 multiply_reduce_fusion.2
  336.5 7.9 convert_reduce_fusion
  356.4 7.6 multiply_reduce_fusion.1
  364.3 5.6 multiply_convert_fusion.1
  369.9 12.2 %copy.87 = bf16[8,4,256,512]{3,2,1,0:T(8,128)(2,1)} copy(bf16[8,4,256,512]{2,3,1,0:T(8,128)(2,1)} %bitcast.281) | data formatting | bytes 16777216 | tf_op jit(solution)/shard_map/reshape | solution.py:165
  382.1 8.7 multiply_convert_fusion
  390.7 12.1 %copy.88 = bf16[8,4,256,512]{3,2,1,0:T(8,128)(2,1)} copy(bf16[8,4,256,512]{2,3,1,0:T(8,128)(2,1)} %bitcast.280) | data formatting | bytes 16777216 | tf_op jit(solution)/shard_map/reshape | solution.py:166
  402.9 14.0 %pad_maximum_fusion = bf16[8,4,256,1024]{3,2,1,0:T(8,128)(2,1)} fusion(bf16[8,4,256,512]{3,2,1,0:T(8,128)(2,1)} %copy.88, bf16[8,4,256,512]{3,2,1,0:T(8,128)(2,1)} %copy.87), kind=kLoop, calls=%fused_computation.1 | loop fusion | flops 33554432 | bytes 33554432 | tf_op jit(solution)/shard_map/concatenate | solution.py:163
  422.6 6.0 multiply_reduce_fusion
  433.6 6.9 convolution_bitcast_fusion.3
  440.5 9.7 %convolution_bitcast_fusion.2 = f32[2048,512]{1,0:T(8,128)} fusion(bf16[4,1,256,512]{3,2,1,0:T(8,128)(2,1)S(1)} %copy-done.21, f32[4]{0:T(128)S(1)} %compare_convert_fusion, f32[4,256,2048]{2,1,0:T(8,128)} %copy-done.59, f32[2048]{0:T(1024)S(1)} %copy-done.57), kind=kOutput, calls=%fused_computation.33 | convolution fusion | flops 2170028032 | bytes 13639696 | tf_op jit(solution)/shard_map/dot_general | solution.py:36
  450.3 158.5 %reduce-scatter.2.cloned.1.call-done = bf16[1,4,256,1024]{3,2,1,0:T(8,128)(2,1)} async-done(((bf16[8,4,256,1024]{3,2,1,0:T(8,128)(2,1)}), bf16[1,4,256,1024]{3,2,1,0:T(8,128)(2,1)}) %reduce-scatter.2.cloned.1.call-update) | async-done | bytes 2097168 | tf_op jit(solution)/shard_map/reduce_scatter | solution.py:162
  608.8 5.1 fusion.17
  648.4 8.1 fusion.52
  658.8 5.8 fusion.16
  673.2 67.9 %all-reduce = (f32[8,512]{1,0:T(8,128)}, f32[1,512]{1,0:T(1,128)S(1)}, f32[1,512]{1,0:T(1,128)S(1)}, f32[1,512]{1,0:T(1,128)S(1)}, f32[1,512]{1,0:T(1,128)S(1)},...) all-reduce(f32[8,512]{1,0:T(8,128)S(1)} %fusion.88, ...), channel_id=1, replica_groups=mesh['tm'=8,'clip'=16] {'tm','clip'}, use_global_device_ids=true, to_apply=%region_20.21 | all-reduce | flops 9216 | bytes 73728 | tf_op jit(solution)/shard_map/psum | solution.py:218
  741.7 128.7 %all-reduce.4.cloned.1.call-done = (f32[512,1536]{1,0:T(8,128)}, f32[512,512]{1,0:T(8,128)}, f32[512,1536]{1,0:T(8,128)}, f32[512,512]{1,0:T(8,128)}, f32[512,2048]{1,0:T(8,128)}, /*index=5*/f32[2048,512]{1,0:T(8,128)}) async-done(((f32[512,1536]{1,0:T(8,128)}, f32[512,512]{1,0:T(8,128)}, f32[512,1536]{1,0:T(8,128)}, f32[512,512]{1,0:T(8,128)}, f32[512,2048]{1,0:T(8,128)}, ...) | async-done | bytes 16777232 | tf_op jit(solution)/shard_map/psum | solution.py:218
  (209 shorter events, 130.8 us)
Async XLA Ops:
  7.2 329.3 %copy-start = (bf16[2048,512]{1,0:T(8,128)(2,1)S(1)}, bf16[2048,512]{1,0:T(8,128)(2,1)}, u32[]{:S(2)}) copy-start(bf16[2048,512]{1,0:T(8,128)(2,1)} %param.26) | copy-start | bytes 6291460
  7.2 7.1 copy-start.14
  8.1 11.2 %copy-start.47 = (f32[1,512]{1,0:T(1,128)}, f32[1,512]{1,0:T(1,128)S(1)}, u32[]{:S(2)}) copy-start(f32[1,512]{1,0:T(1,128)S(1)} %get-tuple-element.76) | copy-start | bytes 6148
  8.9 10.3 %copy-start.49 = (f32[1,512]{1,0:T(1,128)}, f32[1,512]{1,0:T(1,128)S(1)}, u32[]{:S(2)}) copy-start(f32[1,512]{1,0:T(1,128)S(1)} %get-tuple-element.79) | copy-start | bytes 6148
  9.8 26.6 %copy-start.39 = (f32[4,512]{1,0:T(4,128)}, f32[4,512]{1,0:T(4,128)S(1)}, u32[]{:S(2)}) copy-start(f32[4,512]{1,0:T(4,128)S(1)} %fusion.89) | copy-start | bytes 24580
  55.4 235.6 %all-to-all-start = ((bf16[8,4,1,256,1024]{3,4,1,2,0:T(8,128)(2,1)}), bf16[8,4,1,256,1024]{3,4,1,2,0:T(8,128)(2,1)}, u32[]{:S(2)}, u32[]{:S(2)}) async-start(bf16[8,4,1,256,1024]{3,4,1,2,0:T(8,128)(2,1)} %stack.47), calls=%async_computation | async-start | bytes 33554432 | tf_op jit(solution)/shard_map/all_to_all | solution.py:102
  63.6 545.2 %reduce-scatter.2.cloned.1.call-start = ((), (), s32[]{:S(2)}) async-start(), calls=%async_computation.2 | async-start | bytes 18874368 | tf_op jit(solution)/shard_map/reduce_scatter | solution.py:162
  324.8 6.0 copy-start.3
  324.8 6.0 copy-start.36
  331.6 15.6 %copy-start.5 = (f32[4,1,256,512]{3,2,0,1:T(8,128)}, f32[4,1,256,512]{3,2,0,1:T(8,128)S(1)}, u32[]{:S(2)}) copy-start(f32[4,1,256,512]{3,2,0,1:T(8,128)S(1)} %get-tuple-element.86) | copy-start | bytes 6291460
  336.5 8.0 copy-start.59
  356.3 7.6 copy-start.13
  356.3 7.9 copy-start.8
  364.3 5.7 copy-start.25
  369.9 12.2 %copy-start.35 = (f32[4,256,8,8]{1,2,0,3:T(8,128)S(1)}, f32[4,256,8,8]{1,2,0,3:T(8,128)}, u32[]{:S(2)}) copy-start(f32[4,256,8,8]{1,2,0,3:T(8,128)} %convert_convert_fusion) | copy-start | bytes 786436
  416.9 453.6 %all-reduce.4.cloned.1.call-start = ((), (), s32[]{:S(2)}) async-start(), calls=%async_computation.3 | async-start | bytes 33554432 | tf_op jit(solution)/shard_map/psum | solution.py:218
  433.6 6.9 copy-start.21
  608.8 5.1 copy-start.4
  608.8 5.1 copy-start.32
  608.8 5.1 copy-start.53
  613.9 4.9 copy-start.11
  625.5 4.9 copy-start.7
  625.5 9.4 %slice-start = ((s8[8388608]{0:T(1024)(128)(4,1)}), s8[4194304]{0:T(1024)(128)(4,1)S(1)}, s32[]{:S(2)}) async-start(s8[8388608]{0:T(1024)(128)(4,1)} %bitcast.277), calls=%async_computation.4 | async-start | bytes 8388608
  870.4 4.9 copy-start.22
  (41 other events, 98.3 us)
Sparse Core Ops, SparseCore 0:
  417.0 191.7 reduce-scatter.1
  646.7 223.6 all-reduce.3
